TPU v7x, 32 devices: a whole 2x2x4 slice. The times are simulated.
32 devices in a mesh: seq: 8 (over z, y), head: 4 (over x, core).
Axes of the slice: x: 2, y: 2, z: 4, core: 2. Of those that a mesh axis runs over, the one named last changes fastest.
Arguments:
- queries: bfloat16 [1024, 4096], P(('seq', 'head')), may hold values from -6 to 6
- key_vectors: bfloat16 [1024, 4096], P(('seq', 'head')), may hold values from -6 to 6
- value_vectors: bfloat16 [1024, 4096], P(('seq', 'head')), may hold values from -6 to 6
- out_cotangent: bfloat16 [1024, 4096], P(('seq', 'head')), may hold values from -6 to 6
- block_mask: int32 [8, 4], replicated, may hold values from 0 to 1, as said below
Outputs:
- attended: bfloat16 [1024, 4096], P(('seq', 'head'))
- query_grad: bfloat16 [1024, 4096], P(('seq', 'head'))
- key_grad: bfloat16 [1024, 4096], P(('seq', 'head'))
- value_grad: bfloat16 [1024, 4096], P(('seq', 'head'))
Inputs may be any that keep to these rules, and one draw needn't show every extreme that they name: `block_mask`: column 0 is 1 in every row; entry [b, j] with j >= 1 is 0 where b < 2**(j-1).
All inputs are finite; a program needn't handle non-finite values.
Results may differ from a plain program's by a relative error of at most 0.035.
Values may be sent and summed in bfloat16 or wider, within the bound.
A program may use at most 64 MiB of HBM per device.

v0:
```python
import jax
import jax.numpy as jnp
from jax import lax
from jax.sharding import PartitionSpec as P

DH = 128
BLK = 128


NEG = -1e30


def from_behind(block, axis, distance):
    devices = range(lax.axis_size(axis))
    route = [(i - distance, i) for i in devices if i - distance in devices]
    return lax.ppermute(block, axis, route)


def pick_block(offset, blocks, own, arrived):
    if offset == 0:
        return own
    if offset <= blocks:
        joined = jnp.concatenate([arrived[1], own], axis=0)
        return joined[blocks - offset : 2 * blocks - offset]
    return arrived[offset // blocks]


def shards(queries, key_vectors, value_vectors, out_cotangent, block_mask):
    seq_count = lax.axis_size("seq")
    seq_index = lax.axis_index("seq")
    head_queries, head_keys, head_values, head_grads = (
        lax.all_to_all(queries, "head", split_axis=1, concat_axis=0, tiled=True),
        lax.all_to_all(key_vectors, "head", split_axis=1, concat_axis=0, tiled=True),
        lax.all_to_all(value_vectors, "head", split_axis=1, concat_axis=0, tiled=True),
        lax.all_to_all(out_cotangent, "head", split_axis=1, concat_axis=0, tiled=True),
    )
    patches = head_queries.shape[0]
    local_heads = head_queries.shape[1] // DH
    blocks = patches // BLK
    block_shape = (blocks, BLK, local_heads, DH)
    query_own = head_queries.reshape(block_shape)
    key_own = head_keys.reshape(block_shape)
    value_own = head_values.reshape(block_shape)
    grad_own = head_grads.reshape(block_shape)
    columns = block_mask.shape[1]
    offsets = [0] + [2**level for level in range(columns - 1)]
    distances = [2**level for level in range(seq_count.bit_length() - 1)]
    score_scale = DH ** (-0.5)
    my_mask = lax.dynamic_slice_in_dim(block_mask, seq_index * blocks, blocks, 0)
    arrived_keys = {}
    arrived_values = {}
    for distance in distances:
        moved = from_behind((key_own, value_own), "seq", distance)
        arrived_keys[distance] = moved[0]
        arrived_values[distance] = moved[1]
    keys_all = jnp.stack([pick_block(offset, blocks, key_own, arrived_keys) for offset in offsets])
    values_all = jnp.stack(
        [pick_block(offset, blocks, value_own, arrived_values) for offset in offsets]
    )
    position = jnp.arange(BLK)
    causal = position[None, :] <= position[:, None]
    later = jnp.arange(columns)[None, :, None] > 0
    allowed = (my_mask[:, None, None, :, None] == 1) & (
        later[None, None] | causal[None, None, :, None, :]
    )
    scores = (
        jnp.einsum("bqhd,jbkhd->bhqjk", query_own, keys_all, preferred_element_type=jnp.float32)
        * score_scale
    )
    scores = jnp.where(allowed, scores, NEG)
    row_max = jnp.max(scores, axis=(3, 4))
    row_total = jnp.sum(jnp.exp(scores - row_max[..., None, None]), axis=(3, 4))
    log_total = row_max + jnp.log(row_total)
    weights = jnp.exp(scores - log_total[..., None, None])
    rounded = weights.astype(jnp.bfloat16)
    attended = jnp.einsum(
        "bhqjk,jbkhd->bqhd", rounded, values_all, preferred_element_type=jnp.float32
    ).astype(jnp.bfloat16)
    attended_out = lax.all_to_all(
        attended.reshape(patches, local_heads * DH), "head", split_axis=0, concat_axis=1, tiled=True
    )
    row_delta = jnp.einsum("bqhd,bqhd->bhq", grad_own, attended, preferred_element_type=jnp.float32)
    grad_weights = jnp.einsum(
        "bqhd,jbkhd->bhqjk", grad_own, values_all, preferred_element_type=jnp.float32
    )
    grad_scores = (weights * (grad_weights - row_delta[..., None, None]) * score_scale).astype(
        jnp.bfloat16
    )
    query_grad = jnp.einsum(
        "bhqjk,jbkhd->bqhd", grad_scores, keys_all, preferred_element_type=jnp.float32
    ).astype(jnp.bfloat16)
    key_parts = jnp.einsum(
        "bhqjk,bqhd->jbkhd", grad_scores, query_own, preferred_element_type=jnp.float32
    )
    value_parts = jnp.einsum(
        "bhqjk,bqhd->jbkhd", rounded, grad_own, preferred_element_type=jnp.float32
    )
    key_grad = key_parts[0]
    value_grad = value_parts[0]
    near_keys = jnp.zeros((2 * blocks,) + block_shape[1:], jnp.float32)
    near_values = jnp.zeros((2 * blocks,) + block_shape[1:], jnp.float32)
    outgoing_keys = {}
    outgoing_values = {}
    for column in range(1, columns):
        offset = offsets[column]
        if offset <= blocks:
            padding = ((blocks - offset, offset), (0, 0), (0, 0), (0, 0))
            near_keys = jnp.pad(key_parts[column], padding)
            near_values = jnp.pad(value_parts[column], padding)
        else:
            outgoing_keys[offset // blocks] = key_parts[column]
            outgoing_values[offset // blocks] = value_parts[column]
    key_grad = key_grad + near_keys[blocks:]
    value_grad = value_grad + near_values[blocks:]
    outgoing_keys[1] = near_keys[:blocks]
    outgoing_values[1] = near_values[:blocks]
    for distance in distances:
        returned = (
            from_behind(outgoing_keys[distance].astype(jnp.bfloat16), "seq", -distance).astype(
                jnp.float32
            ),
            from_behind(outgoing_values[distance].astype(jnp.bfloat16), "seq", -distance).astype(
                jnp.float32
            ),
        )
        key_grad = key_grad + returned[0]
        value_grad = value_grad + returned[1]
    flat = (patches, local_heads * DH)
    grads_out = (
        lax.all_to_all(query_grad.reshape(flat), "head", split_axis=0, concat_axis=1, tiled=True),
        lax.all_to_all(
            key_grad.astype(jnp.bfloat16).reshape(flat),
            "head",
            split_axis=0,
            concat_axis=1,
            tiled=True,
        ),
        lax.all_to_all(
            value_grad.astype(jnp.bfloat16).reshape(flat),
            "head",
            split_axis=0,
            concat_axis=1,
            tiled=True,
        ),
    )
    return (attended_out, grads_out[0], grads_out[1], grads_out[2])


def solution(mesh):
    placed = (
        P(("seq", "head"), None),
        P(("seq", "head"), None),
        P(("seq", "head"), None),
        P(("seq", "head"), None),
        P(),
    )
    return jax.shard_map(
        shards,
        mesh=mesh,
        in_specs=placed,
        out_specs=(
            P(("seq", "head"), None),
            P(("seq", "head"), None),
            P(("seq", "head"), None),
            P(("seq", "head"), None),
        ),
        check_vma=False,
    )
```

profile of v0, /device:TPU:8, one launch (start us, length us, event | category | flops | bytes accessed | tf_op | source)
XLA Modules:
  0.0 147.5 jit_solution(14948864205212044949)
XLA Ops:
  2.4 3.5 %all-to-all-start.2 = ((bf16[32,4,1024]{2,0,1:T(8,128)(2,1)}), bf16[32,4,1024]{2,0,1:T(8,128)(2,1)S(1)}, u32[]{:S(2)}, u32[]{:S(2)}) async-start(bf16[32,4,1024]{2,0,1:T(8,128)(2,1)} %bitcast.175), calls=%async_computation.2 | async-start | bytes 524288 | tf_op jit(solution)/shard_map/all_to_all | solution.py:32
  7.6 4.3 %all-to-all-done.2 = bf16[32,4,1024]{2,0,1:T(8,128)(2,1)S(1)} async-done(((bf16[32,4,1024]{2,0,1:T(8,128)(2,1)}), bf16[32,4,1024]{2,0,1:T(8,128)(2,1)S(1)}, u32[]{:S(2)}, u32[]{:S(2)}) %all-to-all-start.2) | async-done | bytes 262176 | tf_op jit(solution)/shard_map/all_to_all | solution.py:32
  11.9 3.4 %all-to-all-start.1 = ((bf16[32,4,1024]{2,0,1:T(8,128)(2,1)}), bf16[32,4,1024]{2,0,1:T(8,128)(2,1)S(1)}, u32[]{:S(2)}, u32[]{:S(2)}) async-start(bf16[32,4,1024]{2,0,1:T(8,128)(2,1)} %bitcast.176), calls=%async_computation.1 | async-start | bytes 524288 | tf_op jit(solution)/shard_map/all_to_all | solution.py:33
  16.1 5.3 %all-to-all-done.1 = bf16[32,4,1024]{2,0,1:T(8,128)(2,1)S(1)} async-done(((bf16[32,4,1024]{2,0,1:T(8,128)(2,1)}), bf16[32,4,1024]{2,0,1:T(8,128)(2,1)S(1)}, u32[]{:S(2)}, u32[]{:S(2)}) %all-to-all-start.1) | async-done | bytes 262176 | tf_op jit(solution)/shard_map/all_to_all | solution.py:33
  21.3 3.4 %all-to-all-start = ((bf16[32,4,1024]{2,0,1:T(8,128)(2,1)}), bf16[32,4,1024]{2,0,1:T(8,128)(2,1)S(1)}, u32[]{:S(2)}, u32[]{:S(2)}) async-start(bf16[32,4,1024]{2,0,1:T(8,128)(2,1)} %bitcast.177), calls=%async_computation | async-start | bytes 524288 | tf_op jit(solution)/shard_map/all_to_all | solution.py:34
  24.9 4.5 %collective-permute-start.5 = (bf16[1,128,8,128]{3,1,2,0:T(8,128)(2,1)S(1)}, bf16[1,128,8,128]{3,1,2,0:T(8,128)(2,1)S(1)}, u32[]{:S(2)}, u32[]{:S(2)}) collective-permute-start(bf16[1,128,8,128]{3,1,2,0:T(8,128)(2,1)S(1)} %copy.62), channel_id=1, source_target_pairs={{0,16},{4,20},{8,24},{12,28},{1,17},{5,21},{9,25},{13,29},{2,18},{... | collective-permute-start | bytes 786440 | tf_op jit(solution)/shard_map/ppermute | solution.py:16
  29.4 1.9 %collective-permute-start.4 = (bf16[1,128,8,128]{3,1,2,0:T(8,128)(2,1)S(1)}, bf16[1,128,8,128]{3,1,2,0:T(8,128)(2,1)S(1)}, u32[]{:S(2)}, u32[]{:S(2)}) collective-permute-start(bf16[1,128,8,128]{3,1,2,0:T(8,128)(2,1)S(1)} %copy.62), channel_id=1, source_target_pairs={{0,8},{4,12},{8,16},{12,20},{16,24},{20,28},{1,9},{5,13},{9,17},{1... | collective-permute-start | bytes 786440 | tf_op jit(solution)/shard_map/ppermute | solution.py:16
  31.3 3.4 %collective-permute-start.3 = (bf16[1,128,8,128]{3,1,2,0:T(8,128)(2,1)S(1)}, bf16[1,128,8,128]{3,1,2,0:T(8,128)(2,1)S(1)}, u32[]{:S(2)}, u32[]{:S(2)}) collective-permute-start(bf16[1,128,8,128]{3,1,2,0:T(8,128)(2,1)S(1)} %copy.62), channel_id=1, source_target_pairs={{0,4},{4,8},{8,12},{12,16},{16,20},{20,24},{24,28},{1,5},{5,9},{9,... | collective-permute-start | bytes 786440 | tf_op jit(solution)/shard_map/ppermute | solution.py:16
  35.7 3.4 %all-to-all-start.4 = ((bf16[32,4,1024]{2,0,1:T(8,128)(2,1)}), bf16[32,4,1024]{2,0,1:T(8,128)(2,1)S(1)}, u32[]{:S(2)}, u32[]{:S(2)}) async-start(bf16[32,4,1024]{2,0,1:T(8,128)(2,1)} %bitcast.174), calls=%async_computation.4 | async-start | bytes 524288 | tf_op jit(solution)/shard_map/all_to_all | solution.py:35
  40.2 2.0 %collective-permute-start.2 = (bf16[1,128,8,128]{1,3,2,0:T(8,128)(2,1)}, bf16[1,128,8,128]{1,3,2,0:T(8,128)(2,1)}, u32[]{:S(2)}, u32[]{:S(2)}) collective-permute-start(bf16[1,128,8,128]{1,3,2,0:T(8,128)(2,1)} %copy.57), channel_id=1, source_target_pairs={{0,16},{4,20},{8,24},{12,28},{1,17},{5,21},{9,25},{13,29},{2,18},{... | collective-permute-start | bytes 786440 | tf_op jit(solution)/shard_map/ppermute | solution.py:16
  45.2 1.9 %collective-permute-start = (bf16[1,128,8,128]{1,3,2,0:T(8,128)(2,1)}, bf16[1,128,8,128]{1,3,2,0:T(8,128)(2,1)S(1)}, u32[]{:S(2)}, u32[]{:S(2)}) collective-permute-start(bf16[1,128,8,128]{1,3,2,0:T(8,128)(2,1)} %copy.57), channel_id=1, source_target_pairs={{0,4},{4,8},{8,12},{12,16},{16,20},{20,24},{24,28},{1,5},{5,9},{9,... | collective-permute-start | bytes 786440 | tf_op jit(solution)/shard_map/ppermute | solution.py:16
  47.1 5.3 %collective-permute-done.4 = bf16[1,128,8,128]{3,1,2,0:T(8,128)(2,1)S(1)} collective-permute-done((bf16[1,128,8,128]{3,1,2,0:T(8,128)(2,1)S(1)}, bf16[1,128,8,128]{3,1,2,0:T(8,128)(2,1)S(1)}, u32[]{:S(2)}, u32[]{:S(2)}) %collective-permute-start.4) | collective-permute-done | bytes 262176 | tf_op jit(solution)/shard_map/ppermute | solution.py:16
  55.1 3.0 %collective-permute-done.2 = bf16[1,128,8,128]{1,3,2,0:T(8,128)(2,1)} collective-permute-done((bf16[1,128,8,128]{1,3,2,0:T(8,128)(2,1)}, bf16[1,128,8,128]{1,3,2,0:T(8,128)(2,1)}, u32[]{:S(2)}, u32[]{:S(2)}) %collective-permute-start.2) | collective-permute-done | bytes 262176 | tf_op jit(solution)/shard_map/ppermute | solution.py:16
  58.1 5.6 %collective-permute-done.1 = bf16[1,128,8,128]{1,3,2,0:T(8,128)(2,1)} collective-permute-done((bf16[1,128,8,128]{1,3,2,0:T(8,128)(2,1)}, bf16[1,128,8,128]{1,3,2,0:T(8,128)(2,1)}, u32[]{:S(2)}, u32[]{:S(2)}) %collective-permute-start.1) | collective-permute-done | bytes 262176 | tf_op jit(solution)/shard_map/ppermute | solution.py:16
  65.6 2.5 %bitcast_convert_fusion = (f32[8,128,128]{1,2,0:T(8,128)}, bf16[8,128,128]{2,1,0:T(8,128)(2,1)}) fusion(f32[8,128,4,128]{1,3,2,0:T(8,128)S(1)} %get-tuple-element.11, f32[8,128]{1,0:T(8,128)S(1)} %log_add_fusion, bf16[1,1,128,8,128]{2,4,0,3,1:T(8,128)(2,1)} %bitcast.5, bf16[1,1,128,8,128]{2,4,0,3,1:T(8,128)(2,1)} %bitcast.4, ...), kind=kOutput, calls=%fused_computation.37 | convolution fusion | flops 137101312 | bytes 3936256 | tf_op jit(solution)/shard_map/bhqjk,jbkhd->bqhd/dot_general | solution.py:76
  77.5 2.1 %collective-permute-start.10 = (bf16[1,128,8,128]{3,1,2,0:T(8,128)(2,1)}, bf16[1,128,8,128]{3,1,2,0:T(8,128)(2,1)}, u32[]{:S(2)}, u32[]{:S(2)}) collective-permute-start(bf16[1,128,8,128]{3,1,2,0:T(8,128)(2,1)} %get-tuple-element.6), channel_id=1, source_target_pairs={{8,0},{12,4},{16,8},{20,12},{24,16},{28,20},{9,1},{13,5},{17,9},{2... | collective-permute-start | bytes 786440 | tf_op jit(solution)/shard_map/ppermute | solution.py:16
  85.2 3.4 %all-to-all-start.3 = ((bf16[4,32,1024]{2,1,0:T(8,128)(2,1)}), bf16[4,32,1024]{2,1,0:T(8,128)(2,1)S(1)}, u32[]{:S(2)}, u32[]{:S(2)}) async-start(bf16[4,32,1024]{2,1,0:T(8,128)(2,1)} %all_to_all.113), calls=%async_computation.3 | async-start | bytes 524288 | tf_op jit(solution)/shard_map/all_to_all | solution.py:79
  94.6 3.4 %all-to-all-start.5 = ((bf16[4,32,1024]{2,1,0:T(8,128)(2,1)}), bf16[4,32,1024]{2,1,0:T(8,128)(2,1)S(1)}, u32[]{:S(2)}, u32[]{:S(2)}) async-start(bf16[4,32,1024]{2,1,0:T(8,128)(2,1)} %all_to_all.120), calls=%async_computation.5 | async-start | bytes 524288 | tf_op jit(solution)/shard_map/all_to_all | solution.py:130
  98.1 1.9 %collective-permute-start.7 = (bf16[1,128,8,128]{3,1,2,0:T(8,128)(2,1)}, bf16[1,128,8,128]{3,1,2,0:T(8,128)(2,1)}, u32[]{:S(2)}, u32[]{:S(2)}) collective-permute-start(bf16[1,128,8,128]{3,1,2,0:T(8,128)(2,1)} %get-tuple-element.9), channel_id=1, source_target_pairs={{8,0},{12,4},{16,8},{20,12},{24,16},{28,20},{9,1},{13,5},{17,9},{2... | collective-permute-start | bytes 786440 | tf_op jit(solution)/shard_map/ppermute | solution.py:16
  100.0 13.0 %collective-permute-done.10 = bf16[1,128,8,128]{3,1,2,0:T(8,128)(2,1)} collective-permute-done((bf16[1,128,8,128]{3,1,2,0:T(8,128)(2,1)}, bf16[1,128,8,128]{3,1,2,0:T(8,128)(2,1)}, u32[]{:S(2)}, u32[]{:S(2)}) %collective-permute-start.10) | collective-permute-done | bytes 262176 | tf_op jit(solution)/shard_map/ppermute | solution.py:16
  115.4 3.4 %all-to-all-start.7 = ((bf16[4,32,1024]{2,1,0:T(8,128)(2,1)}), bf16[4,32,1024]{2,1,0:T(8,128)(2,1)S(1)}, u32[]{:S(2)}, u32[]{:S(2)}) async-start(bf16[4,32,1024]{2,1,0:T(8,128)(2,1)} %all_to_all.128), calls=%async_computation.7 | async-start | bytes 524288 | tf_op jit(solution)/shard_map/all_to_all | solution.py:138
  120.7 14.4 %collective-permute-done.7 = bf16[1,128,8,128]{3,1,2,0:T(8,128)(2,1)} collective-permute-done((bf16[1,128,8,128]{3,1,2,0:T(8,128)(2,1)}, bf16[1,128,8,128]{3,1,2,0:T(8,128)(2,1)}, u32[]{:S(2)}, u32[]{:S(2)}) %collective-permute-start.7) | collective-permute-done | bytes 262176 | tf_op jit(solution)/shard_map/ppermute | solution.py:16
  137.3 3.4 %all-to-all-start.6 = ((bf16[4,32,1024]{2,1,0:T(8,128)(2,1)}), bf16[4,32,1024]{2,1,0:T(8,128)(2,1)S(1)}, u32[]{:S(2)}, u32[]{:S(2)}) async-start(bf16[4,32,1024]{2,1,0:T(8,128)(2,1)} %all_to_all.124), calls=%async_computation.6 | async-start | bytes 524288 | tf_op jit(solution)/shard_map/all_to_all | solution.py:131
  142.9 3.8 %all-to-all-done.6 = bf16[4,32,1024]{2,1,0:T(8,128)(2,1)S(1)} async-done(((bf16[4,32,1024]{2,1,0:T(8,128)(2,1)}), bf16[4,32,1024]{2,1,0:T(8,128)(2,1)S(1)}, u32[]{:S(2)}, u32[]{:S(2)}) %all-to-all-start.6) | async-done | bytes 262176 | tf_op jit(solution)/shard_map/all_to_all | solution.py:131
  (89 shorter events, 44.0 us)
Async XLA Ops:
  0.6 14.7 %copy-start = (bf16[32,4096]{1,0:T(8,128)(2,1)S(1)}, bf16[32,4096]{1,0:T(8,128)(2,1)}, u32[]{:S(2)}) copy-start(bf16[32,4096]{1,0:T(8,128)(2,1)} %param.7) | copy-start | bytes 786436
  0.6 34.1 %copy-start.1 = (bf16[32,4096]{1,0:T(8,128)(2,1)S(1)}, bf16[32,4096]{1,0:T(8,128)(2,1)}, u32[]{:S(2)}) copy-start(bf16[32,4096]{1,0:T(8,128)(2,1)} %param.8) | copy-start | bytes 786436
  2.4 33.1 %copy-start.6 = (s32[8,4]{0,1:T(4,128)S(1)}, s32[8,4]{0,1:T(4,128)}, u32[]{:S(2)}) copy-start(s32[8,4]{0,1:T(4,128)} %param.9) | copy-start | bytes 388
  2.4 9.5 %all-to-all-start.2 = ((bf16[32,4,1024]{2,0,1:T(8,128)(2,1)}), bf16[32,4,1024]{2,0,1:T(8,128)(2,1)S(1)}, u32[]{:S(2)}, u32[]{:S(2)}) async-start(bf16[32,4,1024]{2,0,1:T(8,128)(2,1)} %bitcast.175), calls=%async_computation.2 | async-start | bytes 524288 | tf_op jit(solution)/shard_map/all_to_all | solution.py:32
  11.9 9.4 %all-to-all-start.1 = ((bf16[32,4,1024]{2,0,1:T(8,128)(2,1)}), bf16[32,4,1024]{2,0,1:T(8,128)(2,1)S(1)}, u32[]{:S(2)}, u32[]{:S(2)}) async-start(bf16[32,4,1024]{2,0,1:T(8,128)(2,1)} %bitcast.176), calls=%async_computation.1 | async-start | bytes 524288 | tf_op jit(solution)/shard_map/all_to_all | solution.py:33
  21.3 14.4 %all-to-all-start = ((bf16[32,4,1024]{2,0,1:T(8,128)(2,1)}), bf16[32,4,1024]{2,0,1:T(8,128)(2,1)S(1)}, u32[]{:S(2)}, u32[]{:S(2)}) async-start(bf16[32,4,1024]{2,0,1:T(8,128)(2,1)} %bitcast.177), calls=%async_computation | async-start | bytes 524288 | tf_op jit(solution)/shard_map/all_to_all | solution.py:34
  24.9 20.3 %collective-permute-start.5 = (bf16[1,128,8,128]{3,1,2,0:T(8,128)(2,1)S(1)}, bf16[1,128,8,128]{3,1,2,0:T(8,128)(2,1)S(1)}, u32[]{:S(2)}, u32[]{:S(2)}) collective-permute-start(bf16[1,128,8,128]{3,1,2,0:T(8,128)(2,1)S(1)} %copy.62), channel_id=1, source_target_pairs={{0,16},{4,20},{8,24},{12,28},{1,17},{5,21},{9,25},{13,29},{2,18},{... | collective-permute-start | bytes 786440 | tf_op jit(solution)/shard_map/ppermute | solution.py:16
  29.4 23.0 %collective-permute-start.4 = (bf16[1,128,8,128]{3,1,2,0:T(8,128)(2,1)S(1)}, bf16[1,128,8,128]{3,1,2,0:T(8,128)(2,1)S(1)}, u32[]{:S(2)}, u32[]{:S(2)}) collective-permute-start(bf16[1,128,8,128]{3,1,2,0:T(8,128)(2,1)S(1)} %copy.62), channel_id=1, source_target_pairs={{0,8},{4,12},{8,16},{12,20},{16,24},{20,28},{1,9},{5,13},{9,17},{1... | collective-permute-start | bytes 786440 | tf_op jit(solution)/shard_map/ppermute | solution.py:16
  31.3 21.1 %collective-permute-start.3 = (bf16[1,128,8,128]{3,1,2,0:T(8,128)(2,1)S(1)}, bf16[1,128,8,128]{3,1,2,0:T(8,128)(2,1)S(1)}, u32[]{:S(2)}, u32[]{:S(2)}) collective-permute-start(bf16[1,128,8,128]{3,1,2,0:T(8,128)(2,1)S(1)} %copy.62), channel_id=1, source_target_pairs={{0,4},{4,8},{8,12},{12,16},{16,20},{20,24},{24,28},{1,5},{5,9},{9,... | collective-permute-start | bytes 786440 | tf_op jit(solution)/shard_map/ppermute | solution.py:16
  35.7 9.4 %all-to-all-start.4 = ((bf16[32,4,1024]{2,0,1:T(8,128)(2,1)}), bf16[32,4,1024]{2,0,1:T(8,128)(2,1)S(1)}, u32[]{:S(2)}, u32[]{:S(2)}) async-start(bf16[32,4,1024]{2,0,1:T(8,128)(2,1)} %bitcast.174), calls=%async_computation.4 | async-start | bytes 524288 | tf_op jit(solution)/shard_map/all_to_all | solution.py:35
  40.2 17.9 %collective-permute-start.2 = (bf16[1,128,8,128]{1,3,2,0:T(8,128)(2,1)}, bf16[1,128,8,128]{1,3,2,0:T(8,128)(2,1)}, u32[]{:S(2)}, u32[]{:S(2)}) collective-permute-start(bf16[1,128,8,128]{1,3,2,0:T(8,128)(2,1)} %copy.57), channel_id=1, source_target_pairs={{0,16},{4,20},{8,24},{12,28},{1,17},{5,21},{9,25},{13,29},{2,18},{... | collective-permute-start | bytes 786440 | tf_op jit(solution)/shard_map/ppermute | solution.py:16
  42.2 21.5 %collective-permute-start.1 = (bf16[1,128,8,128]{1,3,2,0:T(8,128)(2,1)}, bf16[1,128,8,128]{1,3,2,0:T(8,128)(2,1)}, u32[]{:S(2)}, u32[]{:S(2)}) collective-permute-start(bf16[1,128,8,128]{1,3,2,0:T(8,128)(2,1)} %copy.57), channel_id=1, source_target_pairs={{0,8},{4,12},{8,16},{12,20},{16,24},{20,28},{1,9},{5,13},{9,17},{1... | collective-permute-start | bytes 786440 | tf_op jit(solution)/shard_map/ppermute | solution.py:16
  45.2 20.4 %collective-permute-start = (bf16[1,128,8,128]{1,3,2,0:T(8,128)(2,1)}, bf16[1,128,8,128]{1,3,2,0:T(8,128)(2,1)S(1)}, u32[]{:S(2)}, u32[]{:S(2)}) collective-permute-start(bf16[1,128,8,128]{1,3,2,0:T(8,128)(2,1)} %copy.57), channel_id=1, source_target_pairs={{0,4},{4,8},{8,12},{12,16},{16,20},{20,24},{24,28},{1,5},{5,9},{9,... | collective-permute-start | bytes 786440 | tf_op jit(solution)/shard_map/ppermute | solution.py:16
  74.3 23.8 %collective-permute-start.9 = (bf16[1,128,8,128]{3,1,2,0:T(8,128)(2,1)}, bf16[1,128,8,128]{3,1,2,0:T(8,128)(2,1)}, u32[]{:S(2)}, u32[]{:S(2)}) collective-permute-start(bf16[1,128,8,128]{3,1,2,0:T(8,128)(2,1)} %get-tuple-element.4), channel_id=1, source_target_pairs={{4,0},{8,4},{12,8},{16,12},{20,16},{24,20},{28,24},{5,1},{9,5},{13... | collective-permute-start | bytes 786440 | tf_op jit(solution)/shard_map/ppermute | solution.py:16
  76.2 23.8 %collective-permute-start.11 = (bf16[1,128,8,128]{3,1,2,0:T(8,128)(2,1)}, bf16[1,128,8,128]{3,1,2,0:T(8,128)(2,1)}, u32[]{:S(2)}, u32[]{:S(2)}) collective-permute-start(bf16[1,128,8,128]{3,1,2,0:T(8,128)(2,1)} %get-tuple-element.5), channel_id=1, source_target_pairs={{16,0},{20,4},{24,8},{28,12},{17,1},{21,5},{25,9},{29,13},{18,2},{... | collective-permute-start | bytes 786440 | tf_op jit(solution)/shard_map/ppermute | solution.py:16
  77.5 35.5 %collective-permute-start.10 = (bf16[1,128,8,128]{3,1,2,0:T(8,128)(2,1)}, bf16[1,128,8,128]{3,1,2,0:T(8,128)(2,1)}, u32[]{:S(2)}, u32[]{:S(2)}) collective-permute-start(bf16[1,128,8,128]{3,1,2,0:T(8,128)(2,1)} %get-tuple-element.6), channel_id=1, source_target_pairs={{8,0},{12,4},{16,8},{20,12},{24,16},{28,20},{9,1},{13,5},{17,9},{2... | collective-permute-start | bytes 786440 | tf_op jit(solution)/shard_map/ppermute | solution.py:16
  85.2 9.4 %all-to-all-start.3 = ((bf16[4,32,1024]{2,1,0:T(8,128)(2,1)}), bf16[4,32,1024]{2,1,0:T(8,128)(2,1)S(1)}, u32[]{:S(2)}, u32[]{:S(2)}) async-start(bf16[4,32,1024]{2,1,0:T(8,128)(2,1)} %all_to_all.113), calls=%async_computation.3 | async-start | bytes 524288 | tf_op jit(solution)/shard_map/all_to_all | solution.py:79
  89.5 29.3 %collective-permute-start.6 = (bf16[1,128,8,128]{3,1,2,0:T(8,128)(2,1)}, bf16[1,128,8,128]{3,1,2,0:T(8,128)(2,1)S(1)}, u32[]{:S(2)}, u32[]{:S(2)}) collective-permute-start(bf16[1,128,8,128]{3,1,2,0:T(8,128)(2,1)} %get-tuple-element.7), channel_id=1, source_target_pairs={{4,0},{8,4},{12,8},{16,12},{20,16},{24,20},{28,24},{5,1},{9,5},{13... | collective-permute-start | bytes 786440 | tf_op jit(solution)/shard_map/ppermute | solution.py:16
  91.4 29.3 %collective-permute-start.8 = (bf16[1,128,8,128]{3,1,2,0:T(8,128)(2,1)}, bf16[1,128,8,128]{3,1,2,0:T(8,128)(2,1)}, u32[]{:S(2)}, u32[]{:S(2)}) collective-permute-start(bf16[1,128,8,128]{3,1,2,0:T(8,128)(2,1)} %get-tuple-element.8), channel_id=1, source_target_pairs={{16,0},{20,4},{24,8},{28,12},{17,1},{21,5},{25,9},{29,13},{18,2},{... | collective-permute-start | bytes 786440 | tf_op jit(solution)/shard_map/ppermute | solution.py:16
  94.6 20.8 %all-to-all-start.5 = ((bf16[4,32,1024]{2,1,0:T(8,128)(2,1)}), bf16[4,32,1024]{2,1,0:T(8,128)(2,1)S(1)}, u32[]{:S(2)}, u32[]{:S(2)}) async-start(bf16[4,32,1024]{2,1,0:T(8,128)(2,1)} %all_to_all.120), calls=%async_computation.5 | async-start | bytes 524288 | tf_op jit(solution)/shard_map/all_to_all | solution.py:130
  98.1 37.0 %collective-permute-start.7 = (bf16[1,128,8,128]{3,1,2,0:T(8,128)(2,1)}, bf16[1,128,8,128]{3,1,2,0:T(8,128)(2,1)}, u32[]{:S(2)}, u32[]{:S(2)}) collective-permute-start(bf16[1,128,8,128]{3,1,2,0:T(8,128)(2,1)} %get-tuple-element.9), channel_id=1, source_target_pairs={{8,0},{12,4},{16,8},{20,12},{24,16},{28,20},{9,1},{13,5},{17,9},{2... | collective-permute-start | bytes 786440 | tf_op jit(solution)/shard_map/ppermute | solution.py:16
  115.4 21.9 %all-to-all-start.7 = ((bf16[4,32,1024]{2,1,0:T(8,128)(2,1)}), bf16[4,32,1024]{2,1,0:T(8,128)(2,1)S(1)}, u32[]{:S(2)}, u32[]{:S(2)}) async-start(bf16[4,32,1024]{2,1,0:T(8,128)(2,1)} %all_to_all.128), calls=%async_computation.7 | async-start | bytes 524288 | tf_op jit(solution)/shard_map/all_to_all | solution.py:138
  118.9 16.2 %copy-start.5 = (bf16[1,128,8,128]{3,1,2,0:T(8,128)(2,1)}, bf16[1,128,8,128]{3,1,2,0:T(8,128)(2,1)S(1)}, u32[]{:S(2)}) copy-start(bf16[1,128,8,128]{3,1,2,0:T(8,128)(2,1)S(1)} %collective-permute-done.6) | copy-start | bytes 786436
  137.3 9.4 %all-to-all-start.6 = ((bf16[4,32,1024]{2,1,0:T(8,128)(2,1)}), bf16[4,32,1024]{2,1,0:T(8,128)(2,1)S(1)}, u32[]{:S(2)}, u32[]{:S(2)}) async-start(bf16[4,32,1024]{2,1,0:T(8,128)(2,1)} %all_to_all.124), calls=%async_computation.6 | async-start | bytes 524288 | tf_op jit(solution)/shard_map/all_to_all | solution.py:131
  (11 other events, 44.6 us)
where the time goes:
time: 149 us; the launch traced here: 147 us
  waiting for transfers between devices  60.3 us (40%)
  starting transfers between devices  53.5 us (36%)
  local copies, waits for them, and re-layouts  19.6 us (13%)
  matrix products  9.48 us (6%)
  other arithmetic  3.45 us (2%)
    ppermute x12, waiting for transfers between devices, from_behind(): return lax.ppermute(block, axis, route)  45 us
    ppermute x12, starting transfers between devices, from_behind(): return lax.ppermute(block, axis, route)  26.1 us
    all_to_all x1, waiting for transfers between devices, shards(): lax.all_to_all(key_vectors, 'head', split_axis=1, concat_axis=0, tiled=True)  5.27 us
    all_to_all x1, waiting for transfers between devices, shards(): lax.all_to_all(queries, 'head', split_axis=1, concat_axis=0, tiled=True)  4.33 us
    all_to_all x1, waiting for transfers between devices, shards(): lax.all_to_all(key_grad.astype(jnp.bfloat16).reshape(flat), 'head', split...  3.84 us
    all_to_all x1, starting transfers between devices, shards(): lax.all_to_all(queries, 'head', split_axis=1, concat_axis=0, tiled=True)  3.54 us
    all_to_all x1, starting transfers between devices, shards(): lax.all_to_all(out_cotangent, 'head', split_axis=1, concat_axis=0, tiled=...  3.42 us
    all_to_all x1, starting transfers between devices, shards(): lax.all_to_all(key_grad.astype(jnp.bfloat16).reshape(flat), 'head', split...  3.41 us
  transfers between devices with their start and end apart: 20, of which 11 were waited for; matrix products, arithmetic and copies ran while one was open for 12% of the time, Pallas kernels for 0%

commit v1 on v0

--- a/solution.py
+++ b/solution.py
@@ -1,6 +1,10 @@
+import functools
+
 import jax
 import jax.numpy as jnp
 from jax import lax
+from jax.experimental import pallas as pl
+from jax.experimental.pallas import tpu as pltpu
 from jax.sharding import PartitionSpec as P
 
 DH = 128
@@ -146,6 +150,235 @@
     return (attended_out, grads_out[0], grads_out[1], grads_out[2])
 
 
+def rows_of(index, size):
+    return pl.ds(pl.multiple_of(index * size, size), size)
+
+
+def fused_kernel(
+    seq_count,
+    head_count,
+    mask_ref,
+    q_ref,
+    k_ref,
+    v_ref,
+    g_ref,
+    out_ref,
+    dq_ref,
+    dk_ref,
+    dv_ref,
+    outbound,
+    inbound,
+    results,
+    landed,
+    key_sum,
+    value_sum,
+    local_sem,
+    send_one,
+    recv_one,
+    send_two,
+    recv_two,
+):
+    devices = seq_count * head_count
+    rows, width = q_ref.shape
+    features = width // devices
+    local_heads = features // DH
+    blocks, columns = mask_ref.shape
+    offsets = [0] + [2**level for level in range(columns - 1)]
+    scale = DH ** (-0.5)
+    me = lax.axis_index("seq") * head_count + lax.axis_index("head")
+
+    def place(index):
+        return (index // head_count, index % head_count)
+
+    loads = [
+        pltpu.make_async_copy(ref, outbound.at[i], local_sem.at[i])
+        for i, ref in enumerate((q_ref, k_ref, v_ref, g_ref))
+    ]
+    for load in loads:
+        load.start()
+
+    barrier = pltpu.get_barrier_semaphore()
+
+    def greet(step, carry):
+        pl.semaphore_signal(
+            barrier,
+            inc=1,
+            device_id=place((me + step) % devices),
+            device_id_type=pl.DeviceIdType.MESH,
+        )
+        return carry
+
+    lax.fori_loop(1, devices, greet, 0)
+    for load in loads:
+        load.wait()
+    pl.semaphore_wait(barrier, devices - 1)
+
+    def peer_of(step):
+        turn = devices // 2 + (1 - 2 * (step % 2)) * ((step + 1) // 2)
+        return (me + turn) % devices
+
+    def first_copy(peer, slot):
+        return pltpu.make_async_remote_copy(
+            src_ref=outbound.at[:, :, rows_of(peer, features)],
+            dst_ref=inbound.at[:, rows_of(slot, rows), :],
+            send_sem=send_one.at[peer],
+            recv_sem=recv_one.at[slot],
+            device_id=place(peer),
+            device_id_type=pl.DeviceIdType.MESH,
+        )
+
+    def second_copy(peer, slot):
+        return pltpu.make_async_remote_copy(
+            src_ref=results.at[:, rows_of(peer, rows), :],
+            dst_ref=landed.at[:, :, rows_of(slot, features)],
+            send_sem=send_two.at[peer],
+            recv_sem=recv_two.at[slot],
+            device_id=place(peer),
+            device_id_type=pl.DeviceIdType.MESH,
+        )
+
+    def start_first(step, carry):
+        first_copy(peer_of(step), me).start()
+        return carry
+
+    lax.fori_loop(0, devices - 1, start_first, 0)
+    inbound[:, rows_of(me, rows), :] = outbound[:, :, rows_of(me, features)]
+
+    def wait_first(step, carry):
+        peer = peer_of(step)
+        copy = first_copy(peer, peer)
+        copy.wait_send()
+        copy.wait_recv()
+        return carry
+
+    lax.fori_loop(0, devices - 1, wait_first, 0)
+
+    query_at = lax.broadcasted_iota(jnp.int32, (BLK, BLK), 0)
+    key_at = lax.broadcasted_iota(jnp.int32, (BLK, BLK), 1)
+    causal = key_at <= query_at
+
+    def dot(a, b, dims):
+        return lax.dot_general(a, b, (dims, ((), ())), preferred_element_type=jnp.float32)
+
+    def attend(block, carry):
+        here = rows_of(block, BLK)
+        sources = [rows_of(jnp.maximum(block - offset, 0), BLK) for offset in offsets]
+        for head in range(local_heads):
+            part = slice(head * DH, (head + 1) * DH)
+            query = inbound[0, here, part]
+            grad = inbound[3, here, part]
+            keys = jnp.concatenate([inbound[1, source, part] for source in sources], axis=0)
+            values = jnp.concatenate([inbound[2, source, part] for source in sources], axis=0)
+            scores = dot(query, keys, ((1,), (1,))) * scale
+            pieces = []
+            for j in range(columns):
+                live = mask_ref[block, j] == 1
+                piece = scores[:, j * BLK : (j + 1) * BLK]
+                if j == 0:
+                    piece = jnp.where(causal, piece, NEG)
+                pieces.append(jnp.where(live, piece, NEG))
+            scores = jnp.concatenate(pieces, axis=1)
+            row_max = jnp.max(scores, axis=1, keepdims=True)
+            raised = jnp.exp(scores - row_max)
+            total = jnp.sum(raised, axis=1, keepdims=True)
+            weights = raised * (1.0 / total)
+            rounded = weights.astype(jnp.bfloat16)
+            attended = dot(rounded, values, ((1,), (0,))).astype(jnp.bfloat16)
+            delta = jnp.sum(
+                grad.astype(jnp.float32) * attended.astype(jnp.float32), axis=1, keepdims=True
+            )
+            grad_weights = dot(grad, values, ((1,), (1,)))
+            grad_scores = (weights * (grad_weights - delta) * scale).astype(jnp.bfloat16)
+            query_grad = dot(grad_scores, keys, ((1,), (0,))).astype(jnp.bfloat16)
+            key_parts = dot(grad_scores, query, ((0,), (0,)))
+            value_parts = dot(rounded, grad, ((0,), (0,)))
+            results[0, here, part] = attended
+            results[1, here, part] = query_grad
+            key_sum[here, part] = key_parts[:BLK]
+            value_sum[here, part] = value_parts[:BLK]
+            for j in range(1, columns):
+                piece = slice(j * BLK, (j + 1) * BLK)
+                key_sum[sources[j], part] += key_parts[piece]
+                value_sum[sources[j], part] += value_parts[piece]
+        return carry
+
+    lax.fori_loop(0, blocks, attend, 0)
+
+    def finish(block, carry):
+        here = rows_of(block, BLK)
+        results[2, here, :] = key_sum[here, :].astype(jnp.bfloat16)
+        results[3, here, :] = value_sum[here, :].astype(jnp.bfloat16)
+        return carry
+
+    lax.fori_loop(0, blocks, finish, 0)
+
+    def start_second(step, carry):
+        second_copy(peer_of(step), me).start()
+        return carry
+
+    lax.fori_loop(0, devices - 1, start_second, 0)
+    landed[:, :, rows_of(me, features)] = results[:, rows_of(me, rows), :]
+
+    def wait_second(step, carry):
+        peer = peer_of(step)
+        copy = second_copy(peer, peer)
+        copy.wait_send()
+        copy.wait_recv()
+        return carry
+
+    lax.fori_loop(0, devices - 1, wait_second, 0)
+    stores = [
+        pltpu.make_async_copy(landed.at[i], ref, local_sem.at[i])
+        for i, ref in enumerate((out_ref, dq_ref, dk_ref, dv_ref))
+    ]
+    for store in stores:
+        store.start()
+    for store in stores:
+        store.wait()
+
+
+def fused(seq_count, head_count, queries, key_vectors, value_vectors, out_cotangent, block_mask):
+    devices = seq_count * head_count
+    rows, width = queries.shape
+    tokens, features = rows * devices, width // devices
+    kind = queries.dtype
+    hbm = pl.BlockSpec(memory_space=pl.ANY)
+    one = jax.ShapeDtypeStruct((rows, width), kind)
+    return pl.pallas_call(
+        functools.partial(fused_kernel, seq_count, head_count),
+        out_shape=(one,) * 4,
+        in_specs=[pl.BlockSpec(memory_space=pltpu.SMEM)] + [hbm] * 4,
+        out_specs=(hbm,) * 4,
+        scratch_shapes=[
+            pltpu.VMEM((4, rows, width), kind),
+            pltpu.VMEM((4, tokens, features), kind),
+            pltpu.VMEM((4, tokens, features), kind),
+            pltpu.VMEM((4, rows, width), kind),
+            pltpu.VMEM((tokens, features), jnp.float32),
+            pltpu.VMEM((tokens, features), jnp.float32),
+            pltpu.SemaphoreType.DMA((4,)),
+            pltpu.SemaphoreType.DMA((devices,)),
+            pltpu.SemaphoreType.DMA((devices,)),
+            pltpu.SemaphoreType.DMA((devices,)),
+            pltpu.SemaphoreType.DMA((devices,)),
+        ],
+        compiler_params=pltpu.CompilerParams(
+            collective_id=0, has_side_effects=True, vmem_limit_bytes=32 * 1024 * 1024
+        ),
+    )(block_mask, queries, key_vectors, value_vectors, out_cotangent)
+
+
+def per_device(seq_count, head_count, queries, key_vectors, value_vectors, out_cotangent, block_mask):
+    heads = queries.shape[1] // DH
+    tokens = queries.shape[0] * seq_count * head_count
+    whole_heads = heads % (seq_count * head_count) == 0
+    if whole_heads and tokens == block_mask.shape[0] * BLK:
+        return fused(
+            seq_count, head_count, queries, key_vectors, value_vectors, out_cotangent, block_mask
+        )
+    return shards(queries, key_vectors, value_vectors, out_cotangent, block_mask)
+
+
 def solution(mesh):
     placed = (
         P(("seq", "head"), None),
@@ -155,7 +388,7 @@
         P(),
     )
     return jax.shard_map(
-        shards,
+        functools.partial(per_device, mesh.shape["seq"], mesh.shape["head"]),
         mesh=mesh,
         in_specs=placed,
         out_specs=(

time: 149 us -> 69.5 us (0.47)
  the two profiles are of different devices: /device:TPU:8 before, /device:TPU:0 now
where the time goes in v1:
time: 69.5 us; the launch traced here: 69.2 us
  Pallas kernels  61.2 us (88%)
  local copies, waits for them, and re-layouts  7.37 us (11%)
    pallas_call x1, Pallas kernels, fused(): pl.pallas_call(functools.partial(fused_kernel, seq_count, head_count), ou...  61.2 us
    unnamed x13, local copies, waits for them, and re-layouts  7.37 us

profile of v1, /device:TPU:0, one launch (start us, length us, event | category | flops | bytes accessed | tf_op | source)
XLA Modules:
  0.0 69.2 jit_solution(15727021326304095609)
XLA Ops:
  0.6 0.8 %copy.9.mask_ref = s32[8,4]{1,0:T(8,128)S(1)} copy(s32[8,4]{0,1:T(4,128)} %param.9) | data formatting | bytes 256 | tf_op args[4]
  1.4 0.0 copy-start
  1.4 0.9 %copy-done = bf16[32,4096]{1,0:T(8,128)(2,1)S(1)} copy-done((bf16[32,4096]{1,0:T(8,128)(2,1)S(1)}, bf16[32,4096]{1,0:T(8,128)(2,1)}, u32[]{:S(2)}) %copy-start) | copy-done | bytes 262168
  2.3 0.0 copy-start.1
  2.3 0.9 %copy-done.1 = bf16[32,4096]{1,0:T(8,128)(2,1)S(1)} copy-done((bf16[32,4096]{1,0:T(8,128)(2,1)S(1)}, bf16[32,4096]{1,0:T(8,128)(2,1)}, u32[]{:S(2)}) %copy-start.1) | copy-done | bytes 262168
  3.3 0.0 copy-start.2
  3.3 0.9 %copy-done.2 = bf16[32,4096]{1,0:T(8,128)(2,1)S(1)} copy-done((bf16[32,4096]{1,0:T(8,128)(2,1)S(1)}, bf16[32,4096]{1,0:T(8,128)(2,1)}, u32[]{:S(2)}) %copy-start.2) | copy-done | bytes 262168
  4.2 0.0 copy-start.3
  4.2 0.9 %copy-done.3 = bf16[32,4096]{1,0:T(8,128)(2,1)S(1)} copy-done((bf16[32,4096]{1,0:T(8,128)(2,1)S(1)}, bf16[32,4096]{1,0:T(8,128)(2,1)}, u32[]{:S(2)}) %copy-start.3) | copy-done | bytes 262168
  5.2 61.2 %shard_map.84 = (bf16[32,4096]{1,0:T(8,128)(2,1)S(1)}, bf16[32,4096]{1,0:T(8,128)(2,1)S(1)}, bf16[32,4096]{1,0:T(8,128)(2,1)S(1)}, bf16[32,4096]{1,0:T(8,128)(2,1)S(1)}) custom-call(s32[8,4]{1,0:T(8,128)S(1)} %copy.9.mask_ref, bf16[32,4096]{1,0:T(8,128)(2,1)S(1)} %copy-done, bf16[32,4096]{1,0:T(8,128)(2,1)S(1)} %copy-done.1, bf16[32,4096]{1,0:T(8,128)(2,1)S(1)} %copy-done.2, ...), custom_call_target="tpu_custom_call" | custom-call | tf_op jit(solution)/shard_map/pallas_call | solution.py:347
  66.4 0.7 %copy.14 = bf16[32,4096]{1,0:T(8,128)(2,1)} copy(bf16[32,4096]{1,0:T(8,128)(2,1)S(1)} %get-tuple-element.8) | data formatting | bytes 524288
  67.1 0.7 %copy.15 = bf16[32,4096]{1,0:T(8,128)(2,1)} copy(bf16[32,4096]{1,0:T(8,128)(2,1)S(1)} %get-tuple-element.9) | data formatting | bytes 524288
  67.8 0.7 %copy.16 = bf16[32,4096]{1,0:T(8,128)(2,1)} copy(bf16[32,4096]{1,0:T(8,128)(2,1)S(1)} %get-tuple-element.10) | data formatting | bytes 524288
  68.5 0.7 %copy.17 = bf16[32,4096]{1,0:T(8,128)(2,1)} copy(bf16[32,4096]{1,0:T(8,128)(2,1)S(1)} %get-tuple-element.11) | data formatting | bytes 524288
Async XLA Ops:
  1.4 0.9 %copy-start = (bf16[32,4096]{1,0:T(8,128)(2,1)S(1)}, bf16[32,4096]{1,0:T(8,128)(2,1)}, u32[]{:S(2)}) copy-start(bf16[32,4096]{1,0:T(8,128)(2,1)} %q_ref.1) | copy-start | bytes 786436
  2.3 0.9 %copy-start.1 = (bf16[32,4096]{1,0:T(8,128)(2,1)S(1)}, bf16[32,4096]{1,0:T(8,128)(2,1)}, u32[]{:S(2)}) copy-start(bf16[32,4096]{1,0:T(8,128)(2,1)} %k_ref.1) | copy-start | bytes 786436
  3.3 0.9 %copy-start.2 = (bf16[32,4096]{1,0:T(8,128)(2,1)S(1)}, bf16[32,4096]{1,0:T(8,128)(2,1)}, u32[]{:S(2)}) copy-start(bf16[32,4096]{1,0:T(8,128)(2,1)} %v_ref.1) | copy-start | bytes 786436
  4.2 0.9 %copy-start.3 = (bf16[32,4096]{1,0:T(8,128)(2,1)S(1)}, bf16[32,4096]{1,0:T(8,128)(2,1)}, u32[]{:S(2)}) copy-start(bf16[32,4096]{1,0:T(8,128)(2,1)} %g_ref.1) | copy-start | bytes 786436

commit v2 on v1

--- a/solution.py
+++ b/solution.py
@@ -162,14 +162,10 @@
     k_ref,
     v_ref,
     g_ref,
-    out_ref,
-    dq_ref,
-    dk_ref,
-    dv_ref,
+    landed,
     outbound,
     inbound,
     results,
-    landed,
     key_sum,
     value_sum,
     local_sem,
@@ -182,7 +178,7 @@
     rows, width = q_ref.shape
     features = width // devices
     local_heads = features // DH
-    blocks, columns = mask_ref.shape
+    columns, blocks = mask_ref.shape
     offsets = [0] + [2**level for level in range(columns - 1)]
     scale = DH ** (-0.5)
     me = lax.axis_index("seq") * head_count + lax.axis_index("head")
@@ -272,7 +268,7 @@
             scores = dot(query, keys, ((1,), (1,))) * scale
             pieces = []
             for j in range(columns):
-                live = mask_ref[block, j] == 1
+                live = mask_ref[j, block] == 1
                 piece = scores[:, j * BLK : (j + 1) * BLK]
                 if j == 0:
                     piece = jnp.where(causal, piece, NEG)
@@ -317,7 +313,12 @@
         return carry
 
     lax.fori_loop(0, devices - 1, start_second, 0)
-    landed[:, :, rows_of(me, features)] = results[:, rows_of(me, rows), :]
+    own = pltpu.make_async_copy(
+        results.at[:, rows_of(me, rows), :],
+        landed.at[:, :, rows_of(me, features)],
+        local_sem.at[0],
+    )
+    own.start()
 
     def wait_second(step, carry):
         peer = peer_of(step)
@@ -327,8 +328,12 @@
         return carry
 
     lax.fori_loop(0, devices - 1, wait_second, 0)
+    own.wait()
+
+
+def hand_out(landed, out_ref, dq_ref, dk_ref, dv_ref, sem):
     stores = [
-        pltpu.make_async_copy(landed.at[i], ref, local_sem.at[i])
+        pltpu.make_async_copy(landed.at[i], ref, sem.at[i])
         for i, ref in enumerate((out_ref, dq_ref, dk_ref, dv_ref))
     ]
     for store in stores:
@@ -342,18 +347,18 @@
     rows, width = queries.shape
     tokens, features = rows * devices, width // devices
     kind = queries.dtype
-    hbm = pl.BlockSpec(memory_space=pl.ANY)
+    hbm = pl.BlockSpec(memory_space=pltpu.HBM)
+    anywhere = pl.BlockSpec(memory_space=pl.ANY)
     one = jax.ShapeDtypeStruct((rows, width), kind)
-    return pl.pallas_call(
+    landed = pl.pallas_call(
         functools.partial(fused_kernel, seq_count, head_count),
-        out_shape=(one,) * 4,
+        out_shape=jax.ShapeDtypeStruct((4, rows, width), kind),
         in_specs=[pl.BlockSpec(memory_space=pltpu.SMEM)] + [hbm] * 4,
-        out_specs=(hbm,) * 4,
+        out_specs=anywhere,
         scratch_shapes=[
             pltpu.VMEM((4, rows, width), kind),
             pltpu.VMEM((4, tokens, features), kind),
             pltpu.VMEM((4, tokens, features), kind),
-            pltpu.VMEM((4, rows, width), kind),
             pltpu.VMEM((tokens, features), jnp.float32),
             pltpu.VMEM((tokens, features), jnp.float32),
             pltpu.SemaphoreType.DMA((4,)),
@@ -363,9 +368,16 @@
             pltpu.SemaphoreType.DMA((devices,)),
         ],
         compiler_params=pltpu.CompilerParams(
-            collective_id=0, has_side_effects=True, vmem_limit_bytes=32 * 1024 * 1024
+            collective_id=0, has_side_effects=True, vmem_limit_bytes=62 * 1024 * 1024
         ),
-    )(block_mask, queries, key_vectors, value_vectors, out_cotangent)
+    )(block_mask.T, queries, key_vectors, value_vectors, out_cotangent)
+    return pl.pallas_call(
+        hand_out,
+        out_shape=(one,) * 4,
+        in_specs=[pl.BlockSpec(memory_space=pltpu.VMEM)],
+        out_specs=(hbm,) * 4,
+        scratch_shapes=[pltpu.SemaphoreType.DMA((4,))],
+    )(landed)
 
 
 def per_device(seq_count, head_count, queries, key_vectors, value_vectors, out_cotangent, block_mask):

time: 69.5 us -> 64.5 us (0.928)
  local copies, waits for them, and re-layouts: 7.37 us -> 0 us
  Pallas kernels: 61.2 us -> 63.7 us
    unnamed x13 -> x0, local copies, waits for them, and re-layouts: 7.37 us -> none
    pallas_call x0 -> x1, Pallas kernels: none -> 2.22 us  [fused(): pl.pallas_call(hand_out, out_shape=(one,) * 4, in_specs=[pl.BlockSpec(mem...]
where the time goes in v2:
time: 64.5 us; the launch traced here: 64.3 us
  Pallas kernels  63.7 us (99%)
    pallas_call x1, Pallas kernels, fused(): pl.pallas_call(functools.partial(fused_kernel, seq_count, head_count), ou...  61.5 us
    pallas_call x1, Pallas kernels, fused(): pl.pallas_call(hand_out, out_shape=(one,) * 4, in_specs=[pl.BlockSpec(mem...  2.22 us

profile of v2, /device:TPU:0, one launch (start us, length us, event | category | flops | bytes accessed | tf_op | source)
XLA Modules:
  0.0 64.3 jit_solution(4941639041450058891)
XLA Ops:
  0.6 61.5 %shard_map.84.landed = bf16[4,32,4096]{2,1,0:T(8,128)(2,1)} custom-call(s32[4,8]{1,0:T(4,128)} %bitcast.1, bf16[32,4096]{1,0:T(8,128)(2,1)} %q_ref.1, bf16[32,4096]{1,0:T(8,128)(2,1)} %k_ref.1, bf16[32,4096]{1,0:T(8,128)(2,1)} %v_ref.1, bf16[32,4096]{1,0:T(8,128)(2,1)} %g_ref.1), custom_call_target="tpu_custom_call" | custom-call | tf_op jit(solution)/shard_map/pallas_call | solution.py:353
  62.1 2.2 %shard_map.85 = (bf16[32,4096]{1,0:T(8,128)(2,1)}, bf16[32,4096]{1,0:T(8,128)(2,1)}, bf16[32,4096]{1,0:T(8,128)(2,1)}, bf16[32,4096]{1,0:T(8,128)(2,1)}) custom-call(bf16[4,32,4096]{2,1,0:T(8,128)(2,1)} %shard_map.84.landed), custom_call_target="tpu_custom_call" | custom-call | tf_op jit(solution)/shard_map/pallas_call | solution.py:374

commit v3 on v0

--- a/solution.py
+++ b/solution.py
@@ -1,6 +1,10 @@
+import functools
+
 import jax
 import jax.numpy as jnp
 from jax import lax
+from jax.experimental import pallas as pl
+from jax.experimental.pallas import tpu as pltpu
 from jax.sharding import PartitionSpec as P
 
 DH = 128
@@ -146,6 +150,320 @@
     return (attended_out, grads_out[0], grads_out[1], grads_out[2])
 
 
+def rows_of(index, size):
+    return pl.ds(pl.multiple_of(index * size, size), size)
+
+
+def fused_kernel(
+    seq_count,
+    head_count,
+    mask_ref,
+    q_ref,
+    k_ref,
+    v_ref,
+    g_ref,
+    landed,
+    returned,
+    outbound,
+    inbound,
+    results,
+    results_back,
+    key_sum,
+    value_sum,
+    local_sem,
+    own_in_sem,
+    own_out_sem,
+    send_in,
+    recv_in,
+    send_out,
+    recv_out,
+):
+    devices = seq_count * head_count
+    half = devices // 2
+    rows, width = q_ref.shape
+    local_heads = width // DH // half
+    columns, blocks = mask_ref.shape
+    half_blocks = blocks // 2
+    half_rows = half * rows
+    offsets = [0] + [2**level for level in range(columns - 1)]
+    scale = DH ** (-0.5)
+    me = lax.axis_index("seq") * head_count + lax.axis_index("head")
+    upper = me // half
+    spot = me % half
+
+    def place(index):
+        return (index // head_count, index % head_count)
+
+    loads = [
+        pltpu.make_async_copy(ref, outbound.at[i], local_sem.at[i])
+        for i, ref in enumerate((k_ref, v_ref, q_ref, g_ref))
+    ]
+    for load in loads:
+        load.start()
+
+    barrier = pltpu.get_barrier_semaphore()
+
+    def greet(step, carry):
+        pl.semaphore_signal(
+            barrier,
+            inc=1,
+            device_id=place((me + step) % devices),
+            device_id_type=pl.DeviceIdType.MESH,
+        )
+        return carry
+
+    lax.fori_loop(1, devices, greet, 0)
+
+    @pl.when(upper == 0)
+    def clear():
+        inbound[:, 0:2, 0:half_rows, :] = jnp.zeros(
+            (local_heads, 2, half_rows, DH), inbound.dtype
+        )
+
+    for load in loads:
+        load.wait()
+    pl.semaphore_wait(barrier, devices - 1)
+
+    def near(step):
+        turn = half // 2 + (1 - 2 * (step % 2)) * ((step + 1) // 2)
+        return upper * half + (spot + turn) % half
+
+    def across(step):
+        return (1 - upper) * half + (spot + step) % half
+
+    def copy_in(head, peer, source):
+        return pltpu.make_async_remote_copy(
+            src_ref=outbound.at[:, :, rows_of((peer % half) * local_heads + head, DH)],
+            dst_ref=inbound.at[head, :, rows_of(half + source % half, rows), :],
+            send_sem=send_in.at[head, peer],
+            recv_sem=recv_in.at[head, source],
+            device_id=place(peer),
+            device_id_type=pl.DeviceIdType.MESH,
+        )
+
+    def copy_up(head, peer, source):
+        return pltpu.make_async_remote_copy(
+            src_ref=outbound.at[0:2, :, rows_of((peer % half) * local_heads + head, DH)],
+            dst_ref=inbound.at[head, 0:2, rows_of(source % half, rows), :],
+            send_sem=send_in.at[head, peer],
+            recv_sem=recv_in.at[head, source],
+            device_id=place(peer),
+            device_id_type=pl.DeviceIdType.MESH,
+        )
+
+    def copy_out(head, peer, source):
+        return pltpu.make_async_remote_copy(
+            src_ref=results.at[head, :, rows_of(peer % half, rows), :],
+            dst_ref=landed.at[:, :, rows_of((source % half) * local_heads + head, DH)],
+            send_sem=send_out.at[head, peer],
+            recv_sem=recv_out.at[head, source],
+            device_id=place(peer),
+            device_id_type=pl.DeviceIdType.MESH,
+        )
+
+    def copy_back(head, peer, source):
+        return pltpu.make_async_remote_copy(
+            src_ref=results_back.at[head, :, rows_of(peer % half, rows), :],
+            dst_ref=returned.at[:, :, rows_of((source % half) * local_heads + head, DH)],
+            send_sem=send_out.at[head, peer],
+            recv_sem=recv_out.at[head, source],
+            device_id=place(peer),
+            device_id_type=pl.DeviceIdType.MESH,
+        )
+
+    def own_in(head):
+        return pltpu.make_async_copy(
+            outbound.at[:, :, rows_of(spot * local_heads + head, DH)],
+            inbound.at[head, :, rows_of(half + spot, rows), :],
+            own_in_sem.at[head],
+        )
+
+    def own_out(head):
+        return pltpu.make_async_copy(
+            results.at[head, :, rows_of(spot, rows), :],
+            landed.at[:, :, rows_of(spot * local_heads + head, DH)],
+            own_out_sem.at[head],
+        )
+
+    def each(count, act):
+        def step_of(step, carry):
+            act(step)
+            return carry
+
+        lax.fori_loop(0, count, step_of, 0)
+
+    for head in range(local_heads):
+
+        @pl.when(upper == 0)
+        def send_up():
+            each(half, lambda step: copy_up(head, across(step), me).start())
+
+        each(half - 1, lambda step: copy_in(head, near(step), me).start())
+        own_in(head).start()
+
+    query_at = lax.broadcasted_iota(jnp.int32, (BLK, BLK), 0)
+    key_at = lax.broadcasted_iota(jnp.int32, (BLK, BLK), 1)
+    causal = key_at <= query_at
+
+    def dot(a, b, dims):
+        return lax.dot_general(a, b, (dims, ((), ())), preferred_element_type=jnp.float32)
+
+    def attend(head, block):
+        here = rows_of(block, BLK)
+        own = rows_of(half_blocks + block, BLK)
+        sources = [rows_of(half_blocks + block - offset, BLK) for offset in offsets]
+        query = inbound[head, 2, own, :]
+        grad = inbound[head, 3, own, :]
+        keys = jnp.concatenate([inbound[head, 0, source, :] for source in sources], axis=0)
+        values = jnp.concatenate([inbound[head, 1, source, :] for source in sources], axis=0)
+        scores = dot(query, keys, ((1,), (1,))) * scale
+        pieces = []
+        for j in range(columns):
+            live = mask_ref[j, upper * half_blocks + block] == 1
+            piece = scores[:, j * BLK : (j + 1) * BLK]
+            if j == 0:
+                piece = jnp.where(causal, piece, NEG)
+            pieces.append(jnp.where(live, piece, NEG))
+        scores = jnp.concatenate(pieces, axis=1)
+        row_max = jnp.max(scores, axis=1, keepdims=True)
+        raised = jnp.exp(scores - row_max)
+        total = jnp.sum(raised, axis=1, keepdims=True)
+        weights = raised * (1.0 / total)
+        rounded = weights.astype(jnp.bfloat16)
+        attended = dot(rounded, values, ((1,), (0,))).astype(jnp.bfloat16)
+        delta = jnp.sum(
+            grad.astype(jnp.float32) * attended.astype(jnp.float32), axis=1, keepdims=True
+        )
+        grad_weights = dot(grad, values, ((1,), (1,)))
+        grad_scores = (weights * (grad_weights - delta) * scale).astype(jnp.bfloat16)
+        query_grad = dot(grad_scores, keys, ((1,), (0,))).astype(jnp.bfloat16)
+        key_parts = dot(grad_scores, query, ((0,), (0,)))
+        value_parts = dot(rounded, grad, ((0,), (0,)))
+        results[head, 0, here, :] = attended
+        results[head, 1, here, :] = query_grad
+        key_sum[own, :] = key_parts[:BLK]
+        value_sum[own, :] = value_parts[:BLK]
+        for j in range(1, columns):
+            piece = slice(j * BLK, (j + 1) * BLK)
+            key_sum[sources[j], :] += key_parts[piece]
+            value_sum[sources[j], :] += value_parts[piece]
+
+    for head in range(local_heads):
+        key_sum[0:half_rows, :] = jnp.zeros((half_rows, DH), jnp.float32)
+        value_sum[0:half_rows, :] = jnp.zeros((half_rows, DH), jnp.float32)
+        own_in(head).wait()
+        each(half - 1, lambda step: copy_in(head, near(step), near(step)).wait_recv())
+
+        @pl.when(upper == 1)
+        def await_lower():
+            each(half, lambda step: copy_up(head, across(step), across(step)).wait_recv())
+
+        each(half_blocks, functools.partial(attend, head))
+
+        @pl.when(upper == 1)
+        def send_back():
+            results_back[head, 0] = key_sum[0:half_rows, :].astype(jnp.bfloat16)
+            results_back[head, 1] = value_sum[0:half_rows, :].astype(jnp.bfloat16)
+            each(half, lambda step: copy_back(head, across(step), me).start())
+
+        results[head, 2] = key_sum[half_rows : 2 * half_rows, :].astype(jnp.bfloat16)
+        results[head, 3] = value_sum[half_rows : 2 * half_rows, :].astype(jnp.bfloat16)
+        each(half - 1, lambda step: copy_out(head, near(step), me).start())
+        own_out(head).start()
+
+    for head in range(local_heads):
+        own_out(head).wait()
+
+        def settle(step):
+            peer = near(step)
+            copy_in(head, peer, peer).wait_send()
+            copy = copy_out(head, peer, peer)
+            copy.wait_send()
+            copy.wait_recv()
+
+        each(half - 1, settle)
+
+        @pl.when(upper == 0)
+        def settle_lower():
+            def one(step):
+                peer = across(step)
+                copy_up(head, peer, peer).wait_send()
+                copy_back(head, peer, peer).wait_recv()
+
+            each(half, one)
+
+        @pl.when(upper == 1)
+        def settle_upper():
+            each(half, lambda step: copy_back(head, across(step), across(step)).wait_send())
+
+
+def hand_out(seq_count, landed, returned, out_ref, dq_ref, dk_ref, dv_ref):
+    lower = lax.axis_index("seq") < seq_count // 2
+    out_ref[...] = landed[0]
+    dq_ref[...] = landed[1]
+    for i, ref in enumerate((dk_ref, dv_ref)):
+        own = landed[2 + i]
+        both = own.astype(jnp.float32) + returned[i].astype(jnp.float32)
+        ref[...] = jnp.where(lower, both.astype(own.dtype), own)
+
+
+def fused(seq_count, head_count, queries, key_vectors, value_vectors, out_cotangent, block_mask):
+    devices = seq_count * head_count
+    half = devices // 2
+    rows, width = queries.shape
+    tokens, local_heads = rows * devices, width // DH // half
+    kind = queries.dtype
+    anywhere = pl.BlockSpec(memory_space=pl.ANY)
+    vmem = pl.BlockSpec(memory_space=pltpu.VMEM)
+    one = jax.ShapeDtypeStruct((rows, width), kind)
+    landed, returned = pl.pallas_call(
+        functools.partial(fused_kernel, seq_count, head_count),
+        out_shape=(
+            jax.ShapeDtypeStruct((4, rows, width), kind),
+            jax.ShapeDtypeStruct((2, rows, width), kind),
+        ),
+        in_specs=[pl.BlockSpec(memory_space=pltpu.SMEM)] + [anywhere] * 4,
+        out_specs=(anywhere,) * 2,
+        scratch_shapes=[
+            pltpu.VMEM((4, rows, width), kind),
+            pltpu.VMEM((local_heads, 4, tokens, DH), kind),
+            pltpu.VMEM((local_heads, 4, tokens // 2, DH), kind),
+            pltpu.VMEM((local_heads, 2, tokens // 2, DH), kind),
+            pltpu.VMEM((tokens, DH), jnp.float32),
+            pltpu.VMEM((tokens, DH), jnp.float32),
+            pltpu.SemaphoreType.DMA((4,)),
+            pltpu.SemaphoreType.DMA((local_heads,)),
+            pltpu.SemaphoreType.DMA((local_heads,)),
+            pltpu.SemaphoreType.DMA((local_heads, devices)),
+            pltpu.SemaphoreType.DMA((local_heads, devices)),
+            pltpu.SemaphoreType.DMA((local_heads, devices)),
+            pltpu.SemaphoreType.DMA((local_heads, devices)),
+        ],
+        compiler_params=pltpu.CompilerParams(
+            collective_id=0, has_side_effects=True, vmem_limit_bytes=62 * 1024 * 1024
+        ),
+    )(block_mask.T, queries, key_vectors, value_vectors, out_cotangent)
+    return pl.pallas_call(
+        functools.partial(hand_out, seq_count),
+        out_shape=(one,) * 4,
+        in_specs=[vmem] * 2,
+        out_specs=(vmem,) * 4,
+    )(landed, returned)
+
+
+def per_device(seq_count, head_count, queries, key_vectors, value_vectors, out_cotangent, block_mask):
+    heads = queries.shape[1] // DH
+    devices = seq_count * head_count
+    tokens = queries.shape[0] * devices
+    blocks, columns = block_mask.shape
+    halves = seq_count % 2 == 0 and blocks % 2 == 0 and tokens == blocks * BLK
+    if halves and heads % (devices // 2) == 0 and 2 ** max(columns - 2, 0) <= blocks // 2:
+        return fused(
+            seq_count, head_count, queries, key_vectors, value_vectors, out_cotangent, block_mask
+        )
+    return shards(queries, key_vectors, value_vectors, out_cotangent, block_mask)
+
+
 def solution(mesh):
     placed = (
         P(("seq", "head"), None),
@@ -155,7 +473,7 @@
         P(),
     )
     return jax.shard_map(
-        shards,
+        functools.partial(per_device, mesh.shape["seq"], mesh.shape["head"]),
         mesh=mesh,
         in_specs=placed,
         out_specs=(

time: 149 us -> 56.7 us (0.38)
  the two profiles are of different devices: /device:TPU:8 before, /device:TPU:0 now
where the time goes in v3:
time: 56.7 us; the launch traced here: 56.5 us
  Pallas kernels  55.8 us (98%)
  between operations  0.64 us (1%)
    pallas_call x1, Pallas kernels, fused(): pl.pallas_call(functools.partial(fused_kernel, seq_count, head_count), ou...  53.5 us
    pallas_call x1, Pallas kernels, fused(): pl.pallas_call(functools.partial(hand_out, seq_count), out_shape=(one,) *...  2.34 us

profile of v3, /device:TPU:0, one launch (start us, length us, event | category | flops | bytes accessed | tf_op | source)
XLA Modules:
  0.0 56.5 jit_solution(14697186550495848166)
XLA Ops:
  0.6 53.5 %shard_map.84 = (bf16[4,32,4096]{2,1,0:T(8,128)(2,1)}, bf16[2,32,4096]{2,1,0:T(8,128)(2,1)}) custom-call(s32[4,8]{1,0:T(4,128)} %bitcast.1, bf16[32,4096]{1,0:T(8,128)(2,1)} %q_ref.1, bf16[32,4096]{1,0:T(8,128)(2,1)} %k_ref.1, bf16[32,4096]{1,0:T(8,128)(2,1)} %v_ref.1, bf16[32,4096]{1,0:T(8,128)(2,1)} %g_ref.1), custom_call_target="tpu_custom_call" | custom-call | tf_op jit(solution)/shard_map/pallas_call | solution.py:419
  54.1 2.3 %shard_map.85 = (bf16[32,4096]{1,0:T(8,128)(2,1)}, bf16[32,4096]{1,0:T(8,128)(2,1)}, bf16[32,4096]{1,0:T(8,128)(2,1)}, bf16[32,4096]{1,0:T(8,128)(2,1)}) custom-call(bf16[4,32,4096]{2,1,0:T(8,128)(2,1)} %get-tuple-element.6.landed, bf16[2,32,4096]{2,1,0:T(8,128)(2,1)} %get-tuple-element.7.returned), custom_call_target="tpu_custom_call" | custom-call | tf_op jit(solution)/shard_map/pallas_call | solution.py:446

commit v4 on v3

--- a/solution.py
+++ b/solution.py
@@ -151,6 +151,8 @@
 
 
 def rows_of(index, size):
+    if isinstance(index, int):
+        return pl.ds(index * size, size)
     return pl.ds(pl.multiple_of(index * size, size), size)
 
 
@@ -225,11 +227,10 @@
     pl.semaphore_wait(barrier, devices - 1)
 
     def near(step):
-        turn = half // 2 + (1 - 2 * (step % 2)) * ((step + 1) // 2)
-        return upper * half + (spot + turn) % half
+        return upper * half + (spot + 1 + step) % half
 
     def across(step):
-        return (1 - upper) * half + (spot + step) % half
+        return (1 - upper) * half + (spot + 1 + step) % half
 
     def copy_in(head, peer, source):
         return pltpu.make_async_remote_copy(
@@ -295,10 +296,18 @@
     for head in range(local_heads):
 
         @pl.when(upper == 0)
-        def send_up():
-            each(half, lambda step: copy_up(head, across(step), me).start())
-
-        each(half - 1, lambda step: copy_in(head, near(step), me).start())
+        def send_both():
+            def two(step):
+                copy_up(head, across(step), me).start()
+                copy_in(head, near(step), me).start()
+
+            each(half - 1, two)
+            copy_up(head, across(half - 1), me).start()
+
+        @pl.when(upper == 1)
+        def send_near():
+            each(half - 1, lambda step: copy_in(head, near(step), me).start())
+
         own_in(head).start()
 
     query_at = lax.broadcasted_iota(jnp.int32, (BLK, BLK), 0)
@@ -358,7 +367,8 @@
         def await_lower():
             each(half, lambda step: copy_up(head, across(step), across(step)).wait_recv())
 
-        each(half_blocks, functools.partial(attend, head))
+        for block in range(half_blocks):
+            attend(head, block)
 
         @pl.when(upper == 1)
         def send_back():

time: 56.7 us -> 54.1 us (0.954)
  Pallas kernels: 55.8 us -> 53.3 us
    pallas_call x1, Pallas kernels: 53.5 us -> 50.9 us  [fused(): pl.pallas_call(functools.partial(fused_kernel, seq_count, head_count), ou...]
where the time goes in v4:
time: 54.1 us; the launch traced here: 53.9 us
  Pallas kernels  53.3 us (99%)
  between operations  0.64 us (1%)
    pallas_call x1, Pallas kernels, fused(): pl.pallas_call(functools.partial(fused_kernel, seq_count, head_count), ou...  50.9 us
    pallas_call x1, Pallas kernels, fused(): pl.pallas_call(functools.partial(hand_out, seq_count), out_shape=(one,) *...  2.34 us

profile of v4, /device:TPU:0, one launch (start us, length us, event | category | flops | bytes accessed | tf_op | source)
XLA Modules:
  0.0 53.9 jit_solution(372356493751215083)
XLA Ops:
  0.6 50.9 %shard_map.84 = (bf16[4,32,4096]{2,1,0:T(8,128)(2,1)}, bf16[2,32,4096]{2,1,0:T(8,128)(2,1)}) custom-call(s32[4,8]{1,0:T(4,128)} %bitcast.1, bf16[32,4096]{1,0:T(8,128)(2,1)} %q_ref.1, bf16[32,4096]{1,0:T(8,128)(2,1)} %k_ref.1, bf16[32,4096]{1,0:T(8,128)(2,1)} %v_ref.1, bf16[32,4096]{1,0:T(8,128)(2,1)} %g_ref.1), custom_call_target="tpu_custom_call" | custom-call | tf_op jit(solution)/shard_map/pallas_call | solution.py:429
  51.6 2.3 %shard_map.85 = (bf16[32,4096]{1,0:T(8,128)(2,1)}, bf16[32,4096]{1,0:T(8,128)(2,1)}, bf16[32,4096]{1,0:T(8,128)(2,1)}, bf16[32,4096]{1,0:T(8,128)(2,1)}) custom-call(bf16[4,32,4096]{2,1,0:T(8,128)(2,1)} %get-tuple-element.6.landed, bf16[2,32,4096]{2,1,0:T(8,128)(2,1)} %get-tuple-element.7.returned), custom_call_target="tpu_custom_call" | custom-call | tf_op jit(solution)/shard_map/pallas_call | solution.py:456
